TPU v7x, 32 devices: a whole 2x2x4 slice. The times are simulated.
32 devices in a mesh: fsdp: 8 (over z, y), rep: 4 (over x, core).
Axes of the slice: x: 2, y: 2, z: 4, core: 2. Of those that a mesh axis runs over, the one named last changes fastest.
Arguments:
- tokens: bfloat16 [8192, 1088], P(('fsdp', 'rep')), may hold values from -6 to 6
- lengths: int32 [32, 4], P(('fsdp', 'rep')), may hold values from 0 to 256, as said below
- attn_weights: bfloat16 [4352, 1088], P(('fsdp', 'rep'))
- vectors: bfloat16 [13056], P(('fsdp', 'rep'))
- up_weights: bfloat16 [4352, 1088], P(('fsdp', 'rep')), may hold values from -0.1875 to 0.1875
- down_weights: bfloat16 [4352, 1088], P(('fsdp', 'rep')), may hold values from -0.09375 to 0.09375
- cotangent: bfloat16 [8192, 1088], P(('fsdp', 'rep')), may hold values from -6 to 6
Outputs:
- out: bfloat16 [8192, 1088], P(('fsdp', 'rep'))
- grad_tokens: bfloat16 [8192, 1088], P(('fsdp', 'rep'))
- grad_attn_weights: float32 [4352, 1088], P(('fsdp', 'rep'))
- grad_vectors: float32 [13056], P(('fsdp', 'rep'))
- grad_up_weights: float32 [4352, 1088], P(('fsdp', 'rep'))
- grad_down_weights: float32 [4352, 1088], P(('fsdp', 'rep'))
Inputs may be any that keep to these rules, and one draw needn't show every extreme that they name: `lengths`: row p gives, in order from slot 0, the sequences packed into the blocks of pack p, which is held by device p of fsdp+rep (fsdp major); a row sums to at most 256 and the slots after its sum are empty; in every draw one row, drawn from the seed, is a single sequence of 256 tokens followed by zeros.
All inputs are finite; a program needn't handle non-finite values.
Results may differ from a plain program's by a relative error of at most 0.013.
Values may be sent and summed in bfloat16 or wider, within the bound.
A program may use at most 192 MiB of HBM per device.

v0:
```python
import jax
import jax.numpy as jnp
from jax import lax
from jax.sharding import PartitionSpec as P

HEADS = 17
HEAD_DIM = 64
FF = 4352
epsilon = 1e-05
negative = -1e30


def for_sending(shard):
    return jax.tree.map(lambda a: a.astype(jnp.bfloat16) if a.dtype == jnp.float32 else a, shard)


def contract(left, right, left_dim, right_dim):
    return lax.dot_general(
        left, right, (((left_dim,), (right_dim,)), ((), ())), preferred_element_type=jnp.float32
    )


def normalize(values):
    center = values - jnp.mean(values, axis=1, keepdims=True)
    scaled = lax.rsqrt(jnp.mean(center * center, axis=1, keepdims=True) + epsilon)
    return (center * scaled, scaled)


def norm_back(grad_normed, normed, scaled, gain):
    scaled_grad = grad_normed * gain
    return scaled * (
        scaled_grad
        - jnp.mean(scaled_grad, axis=1, keepdims=True)
        - normed * jnp.mean(scaled_grad * normed, axis=1, keepdims=True)
    )


def visible(segment, span_rows):
    row_ids = lax.iota(jnp.int32, span_rows)[:, None]
    col_ids = lax.iota(jnp.int32, segment.shape[0])[None, :]
    same_seg = segment[:, None] == segment[None, :]
    return same_seg & (col_ids <= row_ids)


def split_heads(matrix):
    return matrix.reshape(matrix.shape[0], HEADS, HEAD_DIM).transpose(1, 0, 2)


def join_heads(stacked):
    return stacked.transpose(1, 0, 2).reshape(stacked.shape[1], HEADS * HEAD_DIM)


def by_owner(matrix, outer_count, inner_count):
    slot_count, width = matrix.shape
    block_width = width // (outer_count * inner_count)
    return matrix.reshape(slot_count, outer_count, inner_count, block_width).transpose(0, 2, 1, 3)


def head_forward(head_parts, segment, span_rows):
    queries, key_heads, value_heads = head_parts
    factor = HEAD_DIM ** (-0.5)
    allowed = visible(segment, span_rows)
    raw_scores = contract(queries, key_heads, 1, 1)
    scores = jnp.where(allowed, raw_scores * factor, negative)
    row_peak = jnp.max(scores, axis=1, keepdims=True)
    exp_scores = jnp.exp(scores - row_peak)
    row_total = jnp.sum(exp_scores, axis=1, keepdims=True)
    prob_low = (exp_scores / row_total).astype(jnp.bfloat16)
    outputs = [contract(prob_low, value_heads, 1, 0)]
    totals = [row_peak + jnp.log(row_total)]
    return (jnp.concatenate(outputs, axis=0).astype(jnp.bfloat16), jnp.concatenate(totals, axis=0))


def head_backward(head_parts, segment, span_rows):
    queries, key_heads, value_heads, totals, grad_mixed = head_parts
    factor = HEAD_DIM ** (-0.5)
    grad_keys = jnp.zeros(key_heads.shape, jnp.float32)
    grad_values = jnp.zeros(value_heads.shape, jnp.float32)
    allowed = visible(segment, span_rows)
    grad_rows = grad_mixed[0:span_rows]
    raw_scores = contract(queries, key_heads, 1, 1)
    probs = jnp.where(allowed, jnp.exp(raw_scores * factor - totals[0:span_rows]), 0.0)
    grad_probs = contract(grad_rows, value_heads, 1, 1)
    row_delta = jnp.sum(probs * grad_probs, axis=1, keepdims=True)
    grad_scores = (probs * (grad_probs - row_delta) * factor).astype(jnp.bfloat16)
    grad_queries = [contract(grad_scores, key_heads, 1, 0)]
    grad_keys = grad_keys + contract(grad_scores, queries, 0, 0)
    grad_values = grad_values + contract(probs.astype(jnp.bfloat16), grad_rows, 0, 0)
    return (jnp.concatenate(grad_queries, axis=0), grad_keys, grad_values)


def local(tokens, lengths, attn_weights, vectors, up_weights, down_weights, cotangent):
    attn_full, vector_full = (
        lax.all_gather(attn_weights, ("fsdp", "rep"), axis=0, tiled=True),
        lax.all_gather(vectors, ("fsdp", "rep"), axis=0, tiled=True),
    )
    params = vector_full.astype(jnp.float32)
    slot_count, model_width = tokens.shape
    span_rows = min(512, slot_count)
    gain_one = params[0:model_width]
    shift_one = params[model_width : 2 * model_width]
    query_bias = params[2 * model_width : 3 * model_width]
    value_bias = params[3 * model_width : 4 * model_width]
    out_bias = params[4 * model_width : 5 * model_width]
    gain_two = params[5 * model_width : 6 * model_width]
    shift_two = params[6 * model_width : 7 * model_width]
    up_bias = params[7 * model_width : 7 * model_width + FF]
    down_bias = params[7 * model_width + FF :]
    seq_ends = jnp.cumsum(lengths[0])
    positions = lax.iota(jnp.int32, slot_count)
    segment = jnp.sum((positions[:, None] >= seq_ends[None, :]).astype(jnp.int32), axis=1)
    live_rows = (positions < seq_ends[-1]).astype(jnp.float32)[:, None]
    inputs = tokens.astype(jnp.float32)
    normed_one, scaled_one = normalize(inputs)
    hidden_one = (normed_one * gain_one + shift_one).astype(jnp.bfloat16)
    qkv_bias = jnp.concatenate([query_bias, jnp.zeros_like(query_bias), value_bias])
    projected = (contract(hidden_one, attn_full[: 3 * model_width], 1, 1) + qkv_bias).astype(
        jnp.bfloat16
    )
    queries = split_heads(projected[:, :model_width])
    key_heads = split_heads(projected[:, model_width : 2 * model_width])
    value_heads = split_heads(projected[:, 2 * model_width :])

    def attend_forward(head_parts):
        return head_forward(head_parts, segment, span_rows)

    mixed_heads, totals = lax.map(attend_forward, (queries, key_heads, value_heads))
    mixed = join_heads(mixed_heads)
    attended = contract(mixed, attn_full[3 * model_width :], 1, 1) + out_bias
    residual = inputs + attended
    normed_two, scaled_two = normalize(residual)
    hidden_two = (normed_two * gain_two + shift_two).astype(jnp.bfloat16)
    up_full, down_full = (
        lax.all_gather(up_weights, ("fsdp", "rep"), axis=0, tiled=True),
        lax.all_gather(down_weights, ("fsdp", "rep"), axis=0, tiled=True),
    )
    upward = contract(hidden_two, up_full, 1, 1) + up_bias
    activated = jax.nn.gelu(upward, approximate=False).astype(jnp.bfloat16)
    output = (residual + contract(activated, down_full, 1, 0) + down_bias) * live_rows
    up_back, down_back = (
        lax.all_gather(up_weights, ("fsdp", "rep"), axis=0, tiled=True),
        lax.all_gather(down_weights, ("fsdp", "rep"), axis=0, tiled=True),
    )
    grad_output = cotangent.astype(jnp.float32) * live_rows
    grad_down_in = grad_output.astype(jnp.bfloat16)
    grad_down_bias = jnp.sum(grad_down_in.astype(jnp.float32), axis=0)
    grad_act = contract(grad_down_in, down_back, 1, 1)

    def gelu_exact(values):
        return jax.nn.gelu(values, approximate=False)

    grad_upward = jax.vjp(gelu_exact, upward)[1](grad_act)[0]
    grad_up_in = grad_upward.astype(jnp.bfloat16)
    grad_up_bias = jnp.sum(grad_up_in.astype(jnp.float32), axis=0)
    grad_hidden_two = contract(grad_up_in, up_back, 1, 0)
    grad_gain_two = jnp.sum(grad_hidden_two * normed_two, axis=0)
    grad_shift_two = jnp.sum(grad_hidden_two, axis=0)
    grad_residual = grad_output + norm_back(grad_hidden_two, normed_two, scaled_two, gain_two)
    grad_attended = grad_residual.astype(jnp.bfloat16)
    attn_back = lax.all_gather(attn_weights, ("fsdp", "rep"), axis=0, tiled=True)
    grad_out_bias = jnp.sum(grad_attended.astype(jnp.float32), axis=0)
    grad_mixed = contract(grad_attended, attn_back[3 * model_width :], 1, 0).astype(jnp.bfloat16)

    def attend_backward(head_parts):
        return head_backward(head_parts, segment, span_rows)

    grad_q_heads, grad_k_heads, grad_v_heads = lax.map(
        attend_backward, (queries, key_heads, value_heads, totals, split_heads(grad_mixed))
    )
    grad_projected = jnp.concatenate(
        [join_heads(grad_q_heads), join_heads(grad_k_heads), join_heads(grad_v_heads)], axis=1
    ).astype(jnp.bfloat16)
    bias_sums = jnp.sum(grad_projected.astype(jnp.float32), axis=0)
    grad_hidden_one = contract(grad_projected, attn_back[: 3 * model_width], 1, 0)
    grad_gain_one = jnp.sum(grad_hidden_one * normed_one, axis=0)
    grad_shift_one = jnp.sum(grad_hidden_one, axis=0)
    grad_inputs = grad_residual + norm_back(grad_hidden_one, normed_one, scaled_one, gain_one)
    outer_count = lax.axis_size("fsdp")
    inner_count = lax.axis_size("rep")
    inner_index = lax.axis_index("rep")
    attn_left = jnp.concatenate([grad_projected, grad_attended], axis=1)
    attn_block = attn_left.shape[1] // (outer_count * inner_count)
    unit_block = grad_up_in.shape[1] // (outer_count * inner_count)
    bundle = jnp.concatenate(
        [
            by_owner(attn_left, outer_count, inner_count),
            by_owner(grad_up_in, outer_count, inner_count),
            by_owner(activated, outer_count, inner_count),
        ],
        axis=3,
    )
    bundle_width = bundle.shape[3]
    bundle = bundle.reshape(slot_count, inner_count * outer_count * bundle_width)
    received = lax.all_to_all(bundle, "rep", split_axis=1, concat_axis=0, tiled=True)
    received = received.reshape(received.shape[0], outer_count, bundle_width)
    attn_cols = received[:, :, :attn_block].reshape(received.shape[0], outer_count * attn_block)
    up_cols = received[:, :, attn_block : attn_block + unit_block].reshape(
        received.shape[0], outer_count * unit_block
    )
    act_cols = received[:, :, attn_block + unit_block :].reshape(
        received.shape[0], outer_count * unit_block
    )
    outer_ids = lax.iota(jnp.int32, outer_count)[:, None]
    inner_ids = lax.iota(jnp.int32, attn_block)[None, :]
    feature_ids = ((outer_ids * inner_count + inner_index) * attn_block + inner_ids).reshape(
        outer_count * attn_block
    )
    is_projection = (feature_ids < 3 * model_width)[None, :]
    start_sums = (
        jnp.zeros((outer_count * attn_block, model_width), jnp.float32),
        jnp.zeros((outer_count * unit_block, model_width), jnp.float32),
        jnp.zeros((outer_count * unit_block, model_width), jnp.float32),
    )
    piece_h1 = lax.all_gather(hidden_one, "rep", axis=0, tiled=True)
    piece_mixed = lax.all_gather(for_sending(mixed), "rep", axis=0, tiled=True)
    piece_h2 = lax.all_gather(hidden_two, "rep", axis=0, tiled=True)
    piece_dd = lax.all_gather(grad_down_in, "rep", axis=0, tiled=True)
    zero_low = jnp.zeros_like(attn_cols)
    left_proj = jnp.where(is_projection, attn_cols, zero_low)
    left_out = jnp.where(is_projection, zero_low, attn_cols)
    attn_total = (
        start_sums[0] + contract(left_proj, piece_h1, 0, 0) + contract(left_out, piece_mixed, 0, 0)
    )
    up_total = start_sums[1] + contract(up_cols, piece_h2, 0, 0)
    down_total = start_sums[2] + contract(act_cols, piece_dd, 0, 0)
    attn_shard, up_shard, down_shard = (
        lax.psum_scatter(attn_total, "fsdp", scatter_dimension=0, tiled=True),
        lax.psum_scatter(up_total, "fsdp", scatter_dimension=0, tiled=True),
        lax.psum_scatter(down_total, "fsdp", scatter_dimension=0, tiled=True),
    )
    grad_params = jnp.concatenate(
        [
            grad_gain_one,
            grad_shift_one,
            bias_sums[:model_width],
            bias_sums[2 * model_width :],
            grad_out_bias,
            grad_gain_two,
            grad_shift_two,
            grad_up_bias,
            grad_down_bias,
        ]
    )
    vector_shard = lax.psum_scatter(grad_params, ("fsdp", "rep"), scatter_dimension=0, tiled=True)
    return (
        output.astype(jnp.bfloat16),
        grad_inputs.astype(jnp.bfloat16),
        attn_shard,
        vector_shard,
        up_shard,
        down_shard,
    )


def solution(mesh):
    return jax.shard_map(
        local,
        mesh=mesh,
        in_specs=(
            P(("fsdp", "rep"), None),
            P(("fsdp", "rep"), None),
            P(("fsdp", "rep"), None),
            P(("fsdp", "rep")),
            P(("fsdp", "rep"), None),
            P(("fsdp", "rep"), None),
            P(("fsdp", "rep"), None),
        ),
        out_specs=(
            P(("fsdp", "rep"), None),
            P(("fsdp", "rep"), None),
            P(("fsdp", "rep"), None),
            P(("fsdp", "rep")),
            P(("fsdp", "rep"), None),
            P(("fsdp", "rep"), None),
        ),
        check_vma=False,
    )
```

profile of v0, /device:TPU:0, one launch (start us, length us, event | category | flops | bytes accessed | tf_op | source)
XLA Modules:
  0.0 895.3 jit_solution(2756972596517927532)
XLA Ops:
  10.4 42.8 %all-reduce = bf16[13056]{0:T(1024)(128)(2,1)S(1)} all-reduce(bf16[13056]{0:T(1024)(128)(2,1)S(1)} %dynamic-update-slice), channel_id=1, replica_groups=mesh['fsdp'=8,'rep'=4] {'fsdp','rep'}, use_global_device_ids=true, to_apply=%add | all-reduce | flops 13056 | bytes 52224
  56.5 42.6 %all-gather.8.cloned.1.call-done = bf16[4352,1088]{1,0:T(8,128)(2,1)} async-done(((bf16[136,1088]{1,0:T(8,128)(2,1)}), bf16[4352,1088]{1,0:T(8,128)(2,1)}) %all-gather.8.cloned.1.call-update) | async-done | bytes 9469968 | tf_op jit(solution)/shard_map/all_gather | solution.py:94
  99.2 5.5 fusion.50
  108.4 37.9 %while.26 = (s32[]{:T(128)}, bf16[17,256,64]{1,2,0:T(8,128)(2,1)S(1)}, f32[17,256,1]{1,2,0:T(1,128)S(1)}, s32[256]{0:T(256)S(1)}, bf16[17,256,64]{2,1,0:T(8,128)...) while((s32[]{:T(128)}, bf16[17,256,64]{1,2,0:T(8,128)(2,1)S(1)}, ...), condition=%wide.region_7.8_spmd, body=%wide.region_4.7_spmd.sunk | while | flops 17514240 | bytes 1030233 | solution.py:127
  153.8 31.4 %all-gather.10.cloned.1.call-done = bf16[4352,1088]{1,0:T(8,128)(2,1)} async-done(((bf16[136,1088]{1,0:T(8,128)(2,1)}), bf16[4352,1088]{1,0:T(8,128)(2,1)}) %all-gather.10.cloned.1.call-update) | async-done | bytes 9469968 | tf_op jit(solution)/shard_map/all_gather | solution.py:134
  185.2 10.8 %convolution_add_fusion.1 = f32[256,4352]{1,0:T(8,128)} fusion(bf16[256,1088]{0,1:T(8,128)(2,1)S(1)} %copy-done.11, bf16[4352,1088]{1,0:T(8,128)(2,1)} %all-gather.10.cloned.1.call-done, f32[4352]{0:T(1024)S(1)} %slice.95), kind=kOutput, calls=%fused_computation.61 | convolution fusion | flops 2425421824 | bytes 14500864 | tf_op jit(solution)/shard_map/dot_general | solution.py:18
  196.1 75.4 %all-gather.12.cloned.1.call-done = bf16[4352,1088]{1,0:T(8,128)(2,1)} async-done(((bf16[136,1088]{1,0:T(8,128)(2,1)}), bf16[4352,1088]{1,0:T(8,128)(2,1)}) %all-gather.12.cloned.1.call-update) | async-done | bytes 9469968 | tf_op jit(solution)/shard_map/all_gather | solution.py:135
  271.5 17.2 %convert_reduce_fusion = (f32[4352]{0:T(1024)S(1)}, bf16[256,4352]{1,0:T(8,128)(2,1)S(1)}, f32[256,4352]{1,0:T(8,128)}) fusion(f32[256,4352]{1,0:T(8,128)} %convolution_add_fusion.1, bf16[256,1088]{0,1:T(8,128)(2,1)S(1)} %get-tuple-element.146, bf16[4352,1088]{1,0:T(8,128)(2,1)} %all-gather.12.cloned.1.call-done), kind=kOutput, calls=%fused_computation.69 | convolution fusion | flops 2506747648 | bytes 21185536 | tf_op jit(solution)/shard_map/dot_general | solution.py:18
  288.7 9.0 %multiply_reduce_fusion.1 = (f32[1088]{0:T(1024)S(1)}, f32[256]{0:T(256)S(1)}, f32[256]{0:T(256)S(1)}, f32[1088]{0:T(1024)S(1)}, f32[256,1088]{0,1:T(8,128)S(1)}) fusion(f32[256,1088]{0,1:T(8,128)S(1)} %get-tuple-element.175, f32[256]{0:T(256)S(1)} %add_rsqrt_fusion, f32[256]{0:T(256)S(1)} %broadcast_multiply_fusion.4, f32[1088]{0:T(1024)S(1)} %get-tuple-element.165, ...), kind=kOutput, calls=%fused_computation.117 | convolution fusion | flops 2426811904 | bytes 13943552 | tf_op jit(solution)/shard_map/dot_general | solution.py:18
  302.2 107.8 %while.27 = (s32[]{:T(128)}, bf16[17,256,64]{1,2,0:T(8,128)(2,1)}, bf16[17,256,64]{1,2,0:T(8,128)(2,1)}, bf16[17,256,64]{1,2,0:T(8,128)(2,1)}, s32[256]{0:T(256)...) while((s32[]{:T(128)}, bf16[17,256,64]{1,2,0:T(8,128)(2,1)}, ...), condition=%wide.region_14.15_spmd, body=%wide.region_12.14_spmd.sunk | while | flops 42794752 | bytes 2633841 | solution.py:167
  438.3 88.6 %all-to-all-done = bf16[256,4,3264]{0,2,1:T(8,128)(2,1)} async-done(((bf16[256,4,3264]{0,2,1:T(8,128)(2,1)}), bf16[256,4,3264]{0,2,1:T(8,128)(2,1)}, u32[]{:S(2)}, u32[]{:S(2)}) %all-to-all-start) | async-done | bytes 6684704 | tf_op jit(solution)/shard_map/all_to_all | solution.py:194
  526.9 27.5 %copy.42 = bf16[4,256,3264]{1,0,2:T(4,128)(2,1)} copy(bf16[4,256,3264]{1,2,0:T(8,128)(2,1)} %bitcast.42) | data formatting | bytes 13369344 | tf_op jit(solution)/shard_map/all_to_all | solution.py:194
  554.4 12.7 %reshape.193 = bf16[1024,8,408]{0,2,1:T(8,128)(2,1)} reshape(bf16[4,256,3264]{1,0,2:T(4,128)(2,1)} %copy.42) | data formatting | bytes 13369344 | tf_op jit(solution)/shard_map/reshape | solution.py:195
  567.1 6.2 fusion.87
  573.3 7.6 fusion.93
  583.7 7.8 fusion.92
  591.5 7.4 convolution_add_fusion
  600.5 6.5 fusion.94
  609.0 8.1 fusion.78
  617.2 40.4 %all-reduce.2 = f32[13056]{0:T(1024)S(1)} all-reduce(f32[13056]{0:T(1024)S(1)} %concatenate.21), channel_id=3, replica_groups=mesh['fsdp'=8,'rep'=4] {'fsdp','rep'}, use_global_device_ids=true, to_apply=%region_26.27.clone | all-reduce | flops 13056 | bytes 104448
  661.2 8.7 fusion.62
  669.9 11.4 %reduce-scatter.12.cloned.1.call-done = f32[136,1088]{1,0:T(8,128)} async-done(((f32[1088,1088]{1,0:T(8,128)}), f32[136,1088]{1,0:T(8,128)}) %reduce-scatter.12.cloned.1.call-update) | async-done | bytes 591888
  681.3 103.6 %reduce-scatter.10.cloned.1.call-done = f32[136,1088]{1,0:T(8,128)} async-done(((f32[1088,1088]{1,0:T(8,128)}), f32[136,1088]{1,0:T(8,128)}) %reduce-scatter.10.cloned.1.call-update) | async-done | bytes 591888
  784.9 103.1 %reduce-scatter.14.cloned.1.call-done = f32[136,1088]{1,0:T(8,128)} async-done(((f32[1088,1088]{1,0:T(8,128)}), f32[136,1088]{1,0:T(8,128)}) %reduce-scatter.14.cloned.1.call-update) | async-done | bytes 591888
  (318 shorter events, 205.1 us)
Async XLA Ops:
  7.2 48.9 %copy-start.2 = (bf16[256,1088]{0,1:T(8,128)(2,1)S(1)}, bf16[256,1088]{0,1:T(8,128)(2,1)}, u32[]{:S(2)}) copy-start(bf16[256,1088]{0,1:T(8,128)(2,1)} %param.11) | copy-start | bytes 1671172
  7.2 48.6 %copy-start.18 = (s32[1,4]{1,0:T(1,128)S(1)}, s32[1,4]{1,0:T(1,128)}, u32[]{:S(2)}) copy-start(s32[1,4]{1,0:T(1,128)} %param.12) | copy-start | bytes 52
  7.2 92.0 %all-gather.8.cloned.1.call-start = ((), (), s32[]{:S(2)}) async-start(), calls=%async_computation.4 | async-start | bytes 10340352 | tf_op jit(solution)/shard_map/all_gather | solution.py:94
  7.9 177.3 %all-gather.10.cloned.1.call-start = ((), (), s32[]{:S(2)}) async-start(), calls=%async_computation.5 | async-start | bytes 10340352 | tf_op jit(solution)/shard_map/all_gather | solution.py:134
  8.7 262.8 %all-gather.12.cloned.1.call-start = ((), (), s32[]{:S(2)}) async-start(), calls=%async_computation.6 | async-start | bytes 10340352 | tf_op jit(solution)/shard_map/all_gather | solution.py:135
  9.4 563.9 %all-gather.18.cloned.1.call-start = ((), (), s32[]{:S(2)}) async-start(), calls=%async_computation.9 | async-start | bytes 2785280 | tf_op jit(solution)/shard_map/all_gather | solution.py:216
  56.4 48.2 %copy-start.13 = (bf16[256,1088]{0,1:T(8,128)(2,1)}, bf16[256,1088]{0,1:T(8,128)(2,1)S(1)}, u32[]{:S(2)}) copy-start(bf16[256,1088]{0,1:T(8,128)(2,1)S(1)} %fusion.72) | copy-start | bytes 1671172
  146.4 3.2 copy-start.15
  146.4 3.2 copy-start.17
  149.6 3.9 copy-start.4
  151.0 34.2 %copy-start.11 = (bf16[256,1088]{0,1:T(8,128)(2,1)S(1)}, bf16[256,1088]{0,1:T(8,128)(2,1)}, u32[]{:S(2)}) copy-start(bf16[256,1088]{0,1:T(8,128)(2,1)} %add_convert_fusion.1) | copy-start | bytes 1671172
  151.0 432.7 %all-gather.14.cloned.1.call-start = ((), (), s32[]{:S(2)}) async-start(), calls=%async_computation.7 | async-start | bytes 2785280 | tf_op jit(solution)/shard_map/all_gather | solution.py:214
  151.6 439.8 %all-gather.16.cloned.1.call-start = ((), (), s32[]{:S(2)}) async-start(), calls=%async_computation.8 | async-start | bytes 2785280 | tf_op jit(solution)/shard_map/all_gather | solution.py:215
  153.8 117.7 %copy-start.14 = (bf16[256,1088]{0,1:T(8,128)(2,1)}, bf16[256,1088]{0,1:T(8,128)(2,1)S(1)}, u32[]{:S(2)}) copy-start(bf16[256,1088]{0,1:T(8,128)(2,1)S(1)} %get-tuple-element.146) | copy-start | bytes 1671172
  288.7 9.0 %copy-start.12 = (bf16[256,4352]{1,0:T(8,128)(2,1)}, bf16[256,4352]{1,0:T(8,128)(2,1)S(1)}, u32[]{:S(2)}) copy-start(bf16[256,4352]{1,0:T(8,128)(2,1)S(1)} %get-tuple-element.148) | copy-start | bytes 6684676
  297.7 3.7 copy-start.6
  432.2 94.7 %all-to-all-start = ((bf16[256,4,3264]{0,2,1:T(8,128)(2,1)}), bf16[256,4,3264]{0,2,1:T(8,128)(2,1)}, u32[]{:S(2)}, u32[]{:S(2)}) async-start(bf16[256,4,3264]{0,2,1:T(8,128)(2,1)} %bitcast.152), calls=%async_computation | async-start | bytes 13369344 | tf_op jit(solution)/shard_map/all_to_all | solution.py:194
  437.5 161.4 %all-gather.20.cloned.1.call-start = ((), (), s32[]{:S(2)}) async-start(), calls=%async_computation.10 | async-start | bytes 2785280 | tf_op jit(solution)/shard_map/all_gather | solution.py:217
  438.3 243.0 %reduce-scatter.12.cloned.1.call-start = ((), (), s32[]{:S(2)}) async-start(), calls=%async_computation.12 | async-start | bytes 5640192
  580.9 204.0 %reduce-scatter.10.cloned.1.call-start = ((), (), s32[]{:S(2)}) async-start(), calls=%async_computation.11 | async-start | bytes 5640192
  583.7 7.8 copy-start.9
  598.9 289.1 %reduce-scatter.14.cloned.1.call-start = ((), (), s32[]{:S(2)}) async-start(), calls=%async_computation.13 | async-start | bytes 5640192
  609.0 49.2 %copy-start.5 = (bf16[256,1088]{0,1:T(8,128)(2,1)S(1)}, bf16[256,1088]{0,1:T(8,128)(2,1)}, u32[]{:S(2)}) copy-start(bf16[256,1088]{0,1:T(8,128)(2,1)} %param.17) | copy-start | bytes 1671172
  609.0 49.2 %copy-start.7 = (f32[256,1088]{0,1:T(8,128)S(1)}, f32[256,1088]{0,1:T(8,128)}, u32[]{:S(2)}) copy-start(f32[256,1088]{0,1:T(8,128)} %copy-done.6) | copy-start | bytes 3342340
  (6 other events, 14.9 us)
Sparse Core Ops, SparseCore 0:
  10.9 88.1 all-gather.7
  102.1 83.1 all-gather.9
  188.2 83.2 all-gather.11
  273.4 22.1 all-gather.17
  297.6 23.5 all-gather.13
  422.8 24.7 all-gather.15
  449.2 37.3 all-gather.19
  581.0 100.2 reduce-scatter.11
  686.0 98.9 reduce-scatter.9
  789.0 98.9 reduce-scatter.13
where the time goes:
time: 907 us; the launch traced here: 895 us
  waiting for transfers between devices  460 us (51%)
  matrix products  237 us (26%)
  blocking collectives  83.2 us (9%)
  local copies, waits for them, and re-layouts  66.3 us (7%)
  other arithmetic  27 us (3%)
  between operations  15.1 us (2%)
    dot_general x131, matrix products, contract(): lax.dot_general(left, right, (((left_dim,), (right_dim,)), ((), ())), pre...  237 us
    unnamed x13, waiting for transfers between devices  222 us
    all_to_all x1, waiting for transfers between devices, local(): lax.all_to_all(bundle, 'rep', split_axis=1, concat_axis=0, tiled=True)  88.6 us
    unnamed x2, blocking collectives  83.2 us
    all_gather x1, waiting for transfers between devices, local(): lax.all_gather(down_weights, ('fsdp', 'rep'), axis=0, tiled=True)  75.4 us
    all_gather x1, waiting for transfers between devices, local(): lax.all_gather(attn_weights, ('fsdp', 'rep'), axis=0, tiled=True)  42.6 us
    all_gather x1, waiting for transfers between devices, local(): lax.all_gather(up_weights, ('fsdp', 'rep'), axis=0, tiled=True)  31.4 us
    all_to_all x1, local copies, waits for them, and re-layouts, local(): lax.all_to_all(bundle, 'rep', split_axis=1, concat_axis=0, tiled=True)  27.5 us
  transfers between devices with their start and end apart: 11, of which 7 were waited for; matrix products, arithmetic and copies ran while one was open for 37% of the time, Pallas kernels for 0%

commit v1 on v0

--- a/solution.py
+++ b/solution.py
@@ -191,7 +191,18 @@
     )
     bundle_width = bundle.shape[3]
     bundle = bundle.reshape(slot_count, inner_count * outer_count * bundle_width)
-    received = lax.all_to_all(bundle, "rep", split_axis=1, concat_axis=0, tiled=True)
+    ways, here = (lax.axis_size("rep"), lax.axis_index("rep"))
+    width_2 = bundle.shape[1] // ways
+    lengths_2 = list(bundle.shape)
+    lengths_2[1] = width_2
+    height = lengths_2[0]
+    lengths_2[0] = height * ways
+    received = jnp.zeros(lengths_2, bundle.dtype)
+    for mask in range(ways):
+        part = lax.dynamic_slice_in_dim(bundle, (here ^ mask) * width_2, width_2, axis=1)
+        if mask:
+            part = lax.ppermute(part, "rep", [(d, d ^ mask) for d in range(ways)])
+        received = lax.dynamic_update_slice_in_dim(received, part, (here ^ mask) * height, axis=0)
     received = received.reshape(received.shape[0], outer_count, bundle_width)
     attn_cols = received[:, :, :attn_block].reshape(received.shape[0], outer_count * attn_block)
     up_cols = received[:, :, attn_block : attn_block + unit_block].reshape(

time: 907 us -> 849 us (0.936)
  local copies, waits for them, and re-layouts: 66.3 us -> 39.1 us
  waiting for transfers between devices: 460 us -> 449 us
  matrix products: 237 us -> 227 us
    all_to_all x1 -> x0, waiting for transfers between devices: 88.6 us -> none  [local(): lax.all_to_all(bundle, 'rep', split_axis=1, concat_axis=0, tiled=True)]
    ppermute x0 -> x3, waiting for transfers between devices: none -> 79.8 us  [local(): part = lax.ppermute(part, 'rep', [(d, d ^ mask) for d in range(ways)])]
    all_to_all x1 -> x0, local copies, waits for them, and re-layouts: 27.5 us -> none  [local(): lax.all_to_all(bundle, 'rep', split_axis=1, concat_axis=0, tiled=True)]
    reshape x1 -> x0, local copies, waits for them, and re-layouts: 12.7 us -> none  [local(): received = received.reshape(received.shape[0], outer_count, bundle_width)]
    dot_general x131, matrix products: 237 us -> 227 us  [contract(): lax.dot_general(left, right, (((left_dim,), (right_dim,)), ((), ())), pre...]
  transfers between devices with their start and end apart: 11 -> 13, of which waited for: 7 -> 9; matrix products, arithmetic and copies ran while one was open for 37% -> 34% of each run, Pallas kernels for 0% -> 0%
where the time goes in v1:
time: 849 us; the launch traced here: 841 us
  waiting for transfers between devices  449 us (53%)
  matrix products  227 us (27%)
  blocking collectives  82.5 us (10%)
  local copies, waits for them, and re-layouts  39.1 us (5%)
  other arithmetic  24.5 us (3%)
  between operations  14.9 us (2%)
    dot_general x131, matrix products, contract(): lax.dot_general(left, right, (((left_dim,), (right_dim,)), ((), ())), pre...  227 us
    unnamed x13, waiting for transfers between devices  220 us
    unnamed x2, blocking collectives  82.5 us
    ppermute x3, waiting for transfers between devices, local(): part = lax.ppermute(part, 'rep', [(d, d ^ mask) for d in range(ways)])  79.8 us
    all_gather x1, waiting for transfers between devices, local(): lax.all_gather(down_weights, ('fsdp', 'rep'), axis=0, tiled=True)  75.4 us
    all_gather x1, waiting for transfers between devices, local(): lax.all_gather(attn_weights, ('fsdp', 'rep'), axis=0, tiled=True)  39.7 us
    all_gather x1, waiting for transfers between devices, local(): lax.all_gather(up_weights, ('fsdp', 'rep'), axis=0, tiled=True)  34.4 us
  transfers between devices with their start and end apart: 13, of which 9 were waited for; matrix products, arithmetic and copies ran while one was open for 34% of the time, Pallas kernels for 0%

profile of v1, /device:TPU:0, one launch (start us, length us, event | category | flops | bytes accessed | tf_op | source)
XLA Modules:
  0.0 841.4 jit_solution(13127074362082883518)
XLA Ops:
  13.9 42.8 %all-reduce = bf16[13056]{0:T(1024)(128)(2,1)S(1)} all-reduce(bf16[13056]{0:T(1024)(128)(2,1)S(1)} %dynamic-update-slice), channel_id=1, replica_groups=mesh['fsdp'=8,'rep'=4] {'fsdp','rep'}, use_global_device_ids=true, to_apply=%add | all-reduce | flops 13056 | bytes 52224
  59.1 39.7 %all-gather.8.cloned.1.call-done = bf16[4352,1088]{1,0:T(8,128)(2,1)} async-done(((bf16[136,1088]{1,0:T(8,128)(2,1)}), bf16[4352,1088]{1,0:T(8,128)(2,1)}) %all-gather.8.cloned.1.call-update) | async-done | bytes 9469968 | tf_op jit(solution)/shard_map/all_gather | solution.py:94
  98.8 5.5 fusion.50
  108.8 38.6 %while.26 = (s32[]{:T(128)}, bf16[17,256,64]{1,2,0:T(8,128)(2,1)S(1)}, f32[17,256,1]{1,2,0:T(1,128)S(1)}, s32[256]{0:T(256)S(1)}, bf16[17,256,64]{2,1,0:T(8,128)...) while((s32[]{:T(128)}, bf16[17,256,64]{1,2,0:T(8,128)(2,1)S(1)}, ...), condition=%wide.region_7.8_spmd, body=%wide.region_4.7_spmd.sunk | while | flops 17514240 | bytes 1030241 | solution.py:127
  150.8 34.4 %all-gather.10.cloned.1.call-done = bf16[4352,1088]{1,0:T(8,128)(2,1)} async-done(((bf16[136,1088]{1,0:T(8,128)(2,1)}), bf16[4352,1088]{1,0:T(8,128)(2,1)}) %all-gather.10.cloned.1.call-update) | async-done | bytes 9469968 | tf_op jit(solution)/shard_map/all_gather | solution.py:134
  185.2 10.8 %convolution_add_fusion.1 = f32[256,4352]{1,0:T(8,128)} fusion(bf16[256,1088]{0,1:T(8,128)(2,1)S(1)} %add_convert_fusion.1, bf16[4352,1088]{1,0:T(8,128)(2,1)} %all-gather.10.cloned.1.call-done, f32[4352]{0:T(1024)S(1)} %slice.95), kind=kOutput, calls=%fused_computation.61 | convolution fusion | flops 2425421824 | bytes 14500864 | tf_op jit(solution)/shard_map/dot_general | solution.py:18
  196.0 75.4 %all-gather.12.cloned.1.call-done = bf16[4352,1088]{1,0:T(8,128)(2,1)} async-done(((bf16[136,1088]{1,0:T(8,128)(2,1)}), bf16[4352,1088]{1,0:T(8,128)(2,1)}) %all-gather.12.cloned.1.call-update) | async-done | bytes 9469968 | tf_op jit(solution)/shard_map/all_gather | solution.py:135
  271.4 17.2 %convert_reduce_fusion = (f32[4352]{0:T(1024)S(1)}, bf16[256,4352]{1,0:T(8,128)(2,1)S(1)}, f32[256,4352]{1,0:T(8,128)}) fusion(f32[256,4352]{1,0:T(8,128)} %convolution_add_fusion.1, bf16[256,1088]{0,1:T(8,128)(2,1)S(1)} %copy-done.20, bf16[4352,1088]{1,0:T(8,128)(2,1)} %all-gather.12.cloned.1.call-done), kind=kOutput, calls=%fused_computation.69 | convolution fusion | flops 2506747648 | bytes 21185536 | tf_op jit(solution)/shard_map/dot_general | solution.py:18
  288.6 9.0 %multiply_reduce_fusion.1 = (f32[1088]{0:T(1024)S(1)}, f32[256]{0:T(256)S(1)}, f32[256]{0:T(256)S(1)}, f32[1088]{0:T(1024)S(1)}, f32[256,1088]{0,1:T(8,128)S(1)}) fusion(f32[256,1088]{0,1:T(8,128)S(1)} %get-tuple-element.179, f32[256]{0:T(256)S(1)} %add_rsqrt_fusion, f32[256]{0:T(256)S(1)} %broadcast_multiply_fusion.4, f32[1088]{0:T(1024)S(1)} %get-tuple-element.169, ...), kind=kOutput, calls=%fused_computation.118 | convolution fusion | flops 2426811904 | bytes 13943552 | tf_op jit(solution)/shard_map/dot_general | solution.py:18
  302.2 97.5 %while.27 = (s32[]{:T(128)}, bf16[17,256,64]{1,2,0:T(8,128)(2,1)S(1)}, bf16[17,256,64]{1,2,0:T(8,128)(2,1)}, bf16[17,256,64]{1,2,0:T(8,128)(2,1)}, s32[256]{0:T(...) while((s32[]{:T(128)}, ...), condition=%wide.region_14.15_spmd, body=%wide.region_12.14_spmd.sunk | while | flops 42794752 | bytes 2633849 | solution.py:167
  404.6 4.6 copy.37
  432.1 45.0 %collective-permute-done.1 = bf16[256,3264]{0,1:T(8,128)(2,1)S(1)} collective-permute-done((bf16[256,3264]{0,1:T(8,128)(2,1)}, bf16[256,3264]{0,1:T(8,128)(2,1)S(1)}, u32[]{:S(2)}, u32[]{:S(2)}) %collective-permute-start.1) | collective-permute-done | bytes 1671200 | tf_op jit(solution)/shard_map/ppermute | solution.py:204
  478.5 33.2 %collective-permute-done.2 = bf16[256,3264]{0,1:T(8,128)(2,1)} collective-permute-done((bf16[256,3264]{0,1:T(8,128)(2,1)}, bf16[256,3264]{0,1:T(8,128)(2,1)}, u32[]{:S(2)}, u32[]{:S(2)}) %collective-permute-start.2) | collective-permute-done | bytes 1671200 | tf_op jit(solution)/shard_map/ppermute | solution.py:204
  514.5 6.1 fusion.87
  520.7 7.6 fusion.94
  531.1 7.8 fusion.92
  538.9 7.1 convolution_add_fusion
  547.6 6.5 fusion.93
  556.2 8.3 fusion.78
  564.5 39.7 %all-reduce.2 = f32[13056]{0:T(1024)S(1)} all-reduce(f32[13056]{0:T(1024)S(1)} %concatenate.21), channel_id=3, replica_groups=mesh['fsdp'=8,'rep'=4] {'fsdp','rep'}, use_global_device_ids=true, to_apply=%region_26.27.clone | all-reduce | flops 13056 | bytes 104448
  607.9 8.7 %fusion.62 = bf16[256,1088]{0,1:T(8,128)(2,1)} fusion(f32[256,1088]{0,1:T(8,128)S(1)} %get-tuple-element.179, bf16[256,4352]{1,0:T(8,128)(2,1)S(1)} %copy-done.4, bf16[4352,1088]{1,0:T(8,128)(2,1)} %all-gather.12.cloned.1.call-done, f32[256]{0:T(256)S(1)} %compare_convert_fusion, f32[1088]{0:T(1024)S(1)} %get-tuple-element.168), kind=kOutput, calls=%fused_computation.91 | convolution fusion | flops 2425421824 | bytes 13374720 | tf_op jit(solution)/shard_map/dot_general | solution.py:18
  616.5 11.1 %reduce-scatter.14.cloned.1.call-done = f32[136,1088]{1,0:T(8,128)} async-done(((f32[1088,1088]{1,0:T(8,128)}), f32[136,1088]{1,0:T(8,128)}) %reduce-scatter.14.cloned.1.call-update) | async-done | bytes 591888
  627.6 103.6 %reduce-scatter.10.cloned.1.call-done = f32[136,1088]{1,0:T(8,128)} async-done(((f32[1088,1088]{1,0:T(8,128)}), f32[136,1088]{1,0:T(8,128)}) %reduce-scatter.10.cloned.1.call-update) | async-done | bytes 591888
  731.2 103.1 %reduce-scatter.12.cloned.1.call-done = f32[136,1088]{1,0:T(8,128)} async-done(((f32[1088,1088]{1,0:T(8,128)}), f32[136,1088]{1,0:T(8,128)}) %reduce-scatter.12.cloned.1.call-update) | async-done | bytes 591888
  (333 shorter events, 198.4 us)
Async XLA Ops:
  7.2 6.4 copy-start.22
  7.2 49.5 %copy-start.5 = (bf16[256,1088]{0,1:T(8,128)(2,1)S(1)}, bf16[256,1088]{0,1:T(8,128)(2,1)}, u32[]{:S(2)}) copy-start(bf16[256,1088]{0,1:T(8,128)(2,1)} %param.11) | copy-start | bytes 1671172
  7.2 91.6 %all-gather.8.cloned.1.call-start = ((), (), s32[]{:S(2)}) async-start(), calls=%async_computation.3 | async-start | bytes 10340352 | tf_op jit(solution)/shard_map/all_gather | solution.py:94
  7.9 177.3 %all-gather.10.cloned.1.call-start = ((), (), s32[]{:S(2)}) async-start(), calls=%async_computation.4 | async-start | bytes 10340352 | tf_op jit(solution)/shard_map/all_gather | solution.py:134
  8.7 262.7 %all-gather.12.cloned.1.call-start = ((), (), s32[]{:S(2)}) async-start(), calls=%async_computation.5 | async-start | bytes 10340352 | tf_op jit(solution)/shard_map/all_gather | solution.py:135
  9.4 511.3 %all-gather.20.cloned.1.call-start = ((), (), s32[]{:S(2)}) async-start(), calls=%async_computation.9 | async-start | bytes 2785280 | tf_op jit(solution)/shard_map/all_gather | solution.py:228
  13.5 517.6 %all-gather.14.cloned.1.call-start = ((), (), s32[]{:S(2)}) async-start(), calls=%async_computation.6 | async-start | bytes 2785280 | tf_op jit(solution)/shard_map/all_gather | solution.py:225
  58.3 480.6 %all-gather.16.cloned.1.call-start = ((), (), s32[]{:S(2)}) async-start(), calls=%async_computation.7 | async-start | bytes 2785280 | tf_op jit(solution)/shard_map/all_gather | solution.py:226
  150.7 45.3 %copy-start.18 = (bf16[256,1088]{0,1:T(8,128)(2,1)}, bf16[256,1088]{0,1:T(8,128)(2,1)S(1)}, u32[]{:S(2)}) copy-start(bf16[256,1088]{0,1:T(8,128)(2,1)S(1)} %add_convert_fusion.1) | copy-start | bytes 1671172
  150.7 120.6 %copy-start.20 = (bf16[256,1088]{0,1:T(8,128)(2,1)S(1)}, bf16[256,1088]{0,1:T(8,128)(2,1)}, u32[]{:S(2)}) copy-start(bf16[256,1088]{0,1:T(8,128)(2,1)} %get-tuple-element.146) | copy-start | bytes 1671172
  288.6 9.0 %copy-start.19 = (bf16[256,4352]{1,0:T(8,128)(2,1)}, bf16[256,4352]{1,0:T(8,128)(2,1)S(1)}, u32[]{:S(2)}) copy-start(bf16[256,4352]{1,0:T(8,128)(2,1)S(1)} %get-tuple-element.148) | copy-start | bytes 6684676
  288.6 9.1 %copy-start.7 = (bf16[256,1088]{0,1:T(8,128)(2,1)S(1)}, bf16[256,1088]{0,1:T(8,128)(2,1)}, u32[]{:S(2)}) copy-start(bf16[256,1088]{0,1:T(8,128)(2,1)} %param.17) | copy-start | bytes 1671172
  297.6 3.8 copy-start.9
  399.7 146.6 %all-gather.18.cloned.1.call-start = ((), (), s32[]{:S(2)}) async-start(), calls=%async_computation.8 | async-start | bytes 2785280 | tf_op jit(solution)/shard_map/all_gather | solution.py:227
  404.6 7.1 copy-start.3
  425.4 3.9 collective-permute-start
  425.6 51.5 %collective-permute-start.1 = (bf16[256,3264]{0,1:T(8,128)(2,1)}, bf16[256,3264]{0,1:T(8,128)(2,1)S(1)}, u32[]{:S(2)}, u32[]{:S(2)}) collective-permute-start(bf16[256,3264]{0,1:T(8,128)(2,1)} %get-tuple-element.160), channel_id=1, source_target_pairs={{0,2},{1,3},{2,0},{3,1},{4,6},{5,7},{6,4},{7,5},{8,10},{9,11},{10,... | collective-permute-start | bytes 5013512 | tf_op jit(solution)/shard_map/ppermute | solution.py:204
  427.3 200.3 %reduce-scatter.14.cloned.1.call-start = ((), (), s32[]{:S(2)}) async-start(), calls=%async_computation.12 | async-start | bytes 5640192
  427.5 84.2 %collective-permute-start.2 = (bf16[256,3264]{0,1:T(8,128)(2,1)}, bf16[256,3264]{0,1:T(8,128)(2,1)}, u32[]{:S(2)}, u32[]{:S(2)}) collective-permute-start(bf16[256,3264]{0,1:T(8,128)(2,1)} %get-tuple-element.159), channel_id=1, source_target_pairs={{0,3},{1,2},{2,1},{3,0},{4,7},{5,6},{6,5},{7,4},{8,11},{9,10},{10,... | collective-permute-start | bytes 5013512 | tf_op jit(solution)/shard_map/ppermute | solution.py:204
  528.3 202.9 %reduce-scatter.10.cloned.1.call-start = ((), (), s32[]{:S(2)}) async-start(), calls=%async_computation.10 | async-start | bytes 5640192
  531.1 7.8 copy-start.12
  546.0 288.3 %reduce-scatter.12.cloned.1.call-start = ((), (), s32[]{:S(2)}) async-start(), calls=%async_computation.11 | async-start | bytes 5640192
  556.1 48.8 %copy-start.8 = (bf16[256,1088]{0,1:T(8,128)(2,1)S(1)}, bf16[256,1088]{0,1:T(8,128)(2,1)}, u32[]{:S(2)}) copy-start(bf16[256,1088]{0,1:T(8,128)(2,1)} %param.17) | copy-start | bytes 1671172
  556.2 48.8 %copy-start.10 = (f32[256,1088]{0,1:T(8,128)S(1)}, f32[256,1088]{0,1:T(8,128)}, u32[]{:S(2)}) copy-start(f32[256,1088]{0,1:T(8,128)} %copy-done.9) | copy-start | bytes 3342340
  (12 other events, 25.4 us)
Sparse Core Ops, SparseCore 0:
  10.9 87.7 all-gather.7
  101.7 83.4 all-gather.9
  188.1 83.2 all-gather.11
  273.3 22.1 all-gather.19
  297.5 23.5 all-gather.13
  399.8 22.1 all-gather.15
  427.4 34.1 all-gather.17
  528.4 99.1 reduce-scatter.13
  632.3 98.9 reduce-scatter.9
  735.3 98.9 reduce-scatter.11
